TPU v7x, 32 devices: a whole 2x2x4 slice. The times are simulated.
32 devices in a mesh: dp: 8 (over z, x), sp: 4 (over y, core).
Axes of the slice: x: 2, y: 2, z: 4, core: 2. Of those that a mesh axis runs over, the one named last changes fastest.
Arguments:
- tokens: bfloat16 [512, 32, 768], P('sp', 'dp'), may hold values from -6 to 6
- lengths: int32 [32], P('dp'), may hold values from 1 to 512, as said below
- w_query: bfloat16 [768, 768], replicated, may hold values from -0.21875 to 0.21875
- b_query: bfloat16 [768], replicated, may hold values from -2 to 2
- w_key: bfloat16 [768, 768], replicated, may hold values from -0.21875 to 0.21875
- w_value: bfloat16 [768, 768], replicated, may hold values from -0.21875 to 0.21875
- b_value: bfloat16 [768], replicated, may hold values from -2 to 2
- w_out: bfloat16 [768, 768], replicated, may hold values from -1.75 to 1.75
- b_out: bfloat16 [768], replicated, may hold values from -2 to 2
- gain_attn: bfloat16 [768], replicated, may hold values from 0.5 to 1.5
- shift_attn: bfloat16 [768], replicated, may hold values from -2 to 2
- w_up: bfloat16 [768, 3072], replicated, may hold values from -0.21875 to 0.21875
- b_up: bfloat16 [3072], replicated, may hold values from -3 to 3
- w_down: bfloat16 [3072, 768], replicated, may hold values from -0.109375 to 0.109375
- b_down: bfloat16 [768], replicated, may hold values from -2 to 2
- gain_ffn: bfloat16 [768], replicated, may hold values from 0.5 to 1.5
- shift_ffn: bfloat16 [768], replicated, may hold values from -2 to 2
- cotangent: bfloat16 [512, 32, 768], P('sp', 'dp'), may hold values from -6 to 6
Outputs:
- mixed: bfloat16 [512, 32, 768], P('sp', 'dp')
- grad_tokens: bfloat16 [512, 32, 768], P('sp', 'dp')
- grad_w_query: float32 [768, 768], P('dp')
- grad_b_query: float32 [768], P('dp')
- grad_w_key: float32 [768, 768], P('dp')
- grad_w_value: float32 [768, 768], P('dp')
- grad_b_value: float32 [768], P('dp')
- grad_w_out: float32 [768, 768], P('dp')
- grad_b_out: float32 [768], P('dp')
- grad_gain_attn: float32 [768], P('dp')
- grad_shift_attn: float32 [768], P('dp')
- grad_w_up: float32 [768, 3072], P('dp')
- grad_b_up: float32 [3072], P('dp')
- grad_w_down: float32 [3072, 768], P('dp')
- grad_b_down: float32 [768], P('dp')
- grad_gain_ffn: float32 [768], P('dp')
- grad_shift_ffn: float32 [768], P('dp')
Inputs may be any that keep to these rules, and one draw needn't show every extreme that they name: Each pair's first lengths slots are live keys; in every aligned block of 4 pairs (those of one index of dp) at least one pair has all 512 slots live.
All inputs are finite; a program needn't handle non-finite values.
Results may differ from a plain program's by a relative error of at most 0.018.
Values may be sent and summed in bfloat16 or wider, within the bound.
A program may use at most 192 MiB of HBM per device.

v0:
```python
import jax
import jax.numpy as jnp
from jax import lax
from jax.sharding import PartitionSpec as P

HEADS = 12
HD = 64


def norm_layer(resid, gain, shift):
    center = resid - jnp.mean(resid, axis=-1, keepdims=True)
    spread = jnp.mean(center * center, axis=-1, keepdims=True)
    return center * lax.rsqrt(spread + 1e-05) * gain + shift


def exact_gelu(value):
    return jax.nn.gelu(value, approximate=False)


def project(left, weight):
    return jnp.einsum("spd,de->spe", left, weight, preferred_element_type=jnp.float32)


def back_project(grad_in, weight):
    return jnp.einsum("spe,de->spd", grad_in, weight, preferred_element_type=jnp.float32)


def weight_grad(left, right):
    return jnp.einsum("spd,spe->de", left, right, preferred_element_type=jnp.float32)


def column_sum(grad_in):
    return jnp.sum(grad_in.astype(jnp.float32), axis=(0, 1))


def shards(
    tokens,
    lengths,
    w_query,
    b_query,
    w_key,
    w_value,
    b_value,
    w_out,
    b_out,
    gain_attn,
    shift_attn,
    w_up,
    b_up,
    w_down,
    b_down,
    gain_ffn,
    shift_ffn,
    cotangent,
):
    local_rows, pair_count, model_width = tokens.shape
    score_scale = HD ** (-0.5)
    total_len = local_rows * lax.axis_size("sp")
    queries = (project(tokens, w_query) + b_query.astype(jnp.float32)).astype(jnp.bfloat16)
    keys_local = project(tokens, w_key).astype(jnp.bfloat16)
    values_local = (project(tokens, w_value) + b_value.astype(jnp.float32)).astype(jnp.bfloat16)
    keys_all, values_all = (
        lax.all_gather(keys_local, "sp", axis=0, tiled=True),
        lax.all_gather(values_local, "sp", axis=0, tiled=True),
    )
    query_heads = queries.reshape(local_rows, pair_count, HEADS, HD)
    key_heads = keys_all.reshape(total_len, pair_count, HEADS, HD)
    value_heads = values_all.reshape(total_len, pair_count, HEADS, HD)
    scores = (
        jnp.einsum("iphe,jphe->phij", query_heads, key_heads, preferred_element_type=jnp.float32)
        * score_scale
    )
    key_valid = jnp.arange(total_len)[None, :] < lengths[:, None]
    scores = jnp.where(key_valid[:, None, None, :], scores, -1e30)
    top_score = jnp.max(scores, axis=-1, keepdims=True)
    expo = jnp.exp(scores - top_score)
    row_total = jnp.sum(expo, axis=-1, keepdims=True)
    weights_full = expo / row_total
    probs = weights_full.astype(jnp.bfloat16)
    attended = jnp.einsum("phij,jphe->iphe", probs, value_heads, preferred_element_type=jnp.float32)
    attended_low = attended.reshape(local_rows, pair_count, model_width).astype(jnp.bfloat16)
    branch = project(attended_low, w_out) + b_out.astype(jnp.float32)
    first_sum = tokens.astype(jnp.float32) + branch
    hidden, first_back = jax.vjp(
        norm_layer, first_sum, gain_attn.astype(jnp.float32), shift_attn.astype(jnp.float32)
    )
    hidden_low = hidden.astype(jnp.bfloat16)
    inner = project(hidden_low, w_up) + b_up.astype(jnp.float32)
    activated, gelu_back = jax.vjp(exact_gelu, inner)
    activated_low = activated.astype(jnp.bfloat16)
    second_sum = hidden + project(activated_low, w_down) + b_down.astype(jnp.float32)
    mixed, second_back = jax.vjp(
        norm_layer, second_sum, gain_ffn.astype(jnp.float32), shift_ffn.astype(jnp.float32)
    )
    d_second, grad_gain_ffn, grad_shift_ffn = second_back(cotangent.astype(jnp.float32))
    d_ffn = d_second.astype(jnp.bfloat16)
    grad_down = weight_grad(activated_low, d_ffn)
    grad_bdown = column_sum(d_ffn)
    d_inner = gelu_back(back_project(d_ffn, w_down))[0].astype(jnp.bfloat16)
    grad_up = weight_grad(hidden_low, d_inner)
    grad_bup = column_sum(d_inner)
    d_hidden = d_second + back_project(d_inner, w_up)
    d_first, grad_gain_attn, grad_shift_attn = first_back(d_hidden)
    d_branch = d_first.astype(jnp.bfloat16)
    grad_out = weight_grad(attended_low, d_branch)
    grad_bout = column_sum(d_branch)
    d_attended = back_project(d_branch, w_out).astype(jnp.bfloat16)
    d_att_heads = d_attended.reshape(local_rows, pair_count, HEADS, HD)
    d_probs = jnp.einsum(
        "iphe,jphe->phij", d_att_heads, value_heads, preferred_element_type=jnp.float32
    )
    row_delta = jnp.sum(weights_full * d_probs, axis=-1, keepdims=True)
    d_scores = weights_full * (d_probs - row_delta)
    d_scores_low = d_scores.astype(jnp.bfloat16)
    d_query_heads = (
        jnp.einsum("phij,jphe->iphe", d_scores_low, key_heads, preferred_element_type=jnp.float32)
        * score_scale
    )
    d_queries = d_query_heads.reshape(local_rows, pair_count, model_width).astype(jnp.bfloat16)
    row_count = local_rows * lax.axis_size("sp")
    key_part = (
        jnp.einsum("phij,iphe->jphe", d_scores_low, query_heads, preferred_element_type=jnp.float32)
        * score_scale
    )
    value_part = jnp.einsum(
        "phij,iphe->jphe", probs, d_att_heads, preferred_element_type=jnp.float32
    )
    key_grads = lax.psum_scatter(
        jnp.concatenate(
            (
                key_part.reshape(row_count, pair_count, model_width),
                value_part.reshape(row_count, pair_count, model_width),
            ),
            axis=2,
        ).astype(jnp.bfloat16),
        "sp",
        scatter_dimension=0,
        tiled=True,
    ).astype(jnp.float32)
    d_keys = key_grads[:, :, :model_width].astype(jnp.bfloat16)
    d_values = key_grads[:, :, model_width:].astype(jnp.bfloat16)
    grad_query = weight_grad(tokens, d_queries)
    grad_bquery = column_sum(d_queries)
    grad_key = weight_grad(tokens, d_keys)
    grad_value = weight_grad(tokens, d_values)
    grad_bvalue = column_sum(d_values)
    d_tokens = (
        d_first
        + back_project(d_queries, w_query)
        + back_project(d_keys, w_key)
        + back_project(d_values, w_value)
    )
    summed = (
        lax.psum_scatter(grad_query, "dp", scatter_dimension=0, tiled=True),
        lax.psum_scatter(grad_bquery, "dp", scatter_dimension=0, tiled=True),
        lax.psum_scatter(grad_key, "dp", scatter_dimension=0, tiled=True),
        lax.psum_scatter(grad_value, "dp", scatter_dimension=0, tiled=True),
        lax.psum_scatter(grad_bvalue, "dp", scatter_dimension=0, tiled=True),
        lax.psum_scatter(grad_out, "dp", scatter_dimension=0, tiled=True),
        lax.psum_scatter(grad_bout, "dp", scatter_dimension=0, tiled=True),
        lax.psum_scatter(grad_gain_attn, "dp", scatter_dimension=0, tiled=True),
        lax.psum_scatter(grad_shift_attn, "dp", scatter_dimension=0, tiled=True),
        lax.psum_scatter(grad_up, "dp", scatter_dimension=0, tiled=True),
        lax.psum_scatter(grad_bup, "dp", scatter_dimension=0, tiled=True),
        lax.psum_scatter(grad_down, "dp", scatter_dimension=0, tiled=True),
        lax.psum_scatter(grad_bdown, "dp", scatter_dimension=0, tiled=True),
        lax.psum_scatter(grad_gain_ffn, "dp", scatter_dimension=0, tiled=True),
        lax.psum_scatter(grad_shift_ffn, "dp", scatter_dimension=0, tiled=True),
    )
    summed = tuple(
        (
            lax.psum(summed[0].astype(jnp.bfloat16), "sp").astype(jnp.float32),
            lax.psum(summed[1].astype(jnp.bfloat16), "sp").astype(jnp.float32),
            lax.psum(summed[2].astype(jnp.bfloat16), "sp").astype(jnp.float32),
            lax.psum(summed[3].astype(jnp.bfloat16), "sp").astype(jnp.float32),
            lax.psum(summed[4].astype(jnp.bfloat16), "sp").astype(jnp.float32),
            lax.psum(summed[5].astype(jnp.bfloat16), "sp").astype(jnp.float32),
            lax.psum(summed[6].astype(jnp.bfloat16), "sp").astype(jnp.float32),
            lax.psum(summed[7].astype(jnp.bfloat16), "sp").astype(jnp.float32),
            lax.psum(summed[8].astype(jnp.bfloat16), "sp").astype(jnp.float32),
            lax.psum(summed[9].astype(jnp.bfloat16), "sp").astype(jnp.float32),
            lax.psum(summed[10].astype(jnp.bfloat16), "sp").astype(jnp.float32),
            lax.psum(summed[11].astype(jnp.bfloat16), "sp").astype(jnp.float32),
            lax.psum(summed[12].astype(jnp.bfloat16), "sp").astype(jnp.float32),
            lax.psum(summed[13].astype(jnp.bfloat16), "sp").astype(jnp.float32),
            lax.psum(summed[14].astype(jnp.bfloat16), "sp").astype(jnp.float32),
        )
    )
    return (
        mixed.astype(jnp.bfloat16),
        d_tokens.astype(jnp.bfloat16),
        summed[0],
        summed[1],
        summed[2],
        summed[3],
        summed[4],
        summed[5],
        summed[6],
        summed[7],
        summed[8],
        summed[9],
        summed[10],
        summed[11],
        summed[12],
        summed[13],
        summed[14],
    )


def solution(mesh):
    placed = (
        P("sp", "dp", None),
        P("dp"),
        P(),
        P(),
        P(),
        P(),
        P(),
        P(),
        P(),
        P(),
        P(),
        P(),
        P(),
        P(),
        P(),
        P(),
        P(),
        P("sp", "dp", None),
    )
    return jax.shard_map(
        shards,
        mesh=mesh,
        in_specs=placed,
        out_specs=(
            P("sp", "dp", None),
            P("sp", "dp", None),
            P("dp", None),
            P("dp"),
            P("dp", None),
            P("dp", None),
            P("dp"),
            P("dp", None),
            P("dp"),
            P("dp"),
            P("dp"),
            P("dp", None),
            P("dp"),
            P("dp", None),
            P("dp"),
            P("dp"),
            P("dp"),
        ),
        check_vma=False,
    )
```

profile of v0, /device:TPU:0, one launch (start us, length us, event | category | flops | bytes accessed | tf_op | source)
XLA Modules:
  0.0 936.5 jit_solution(1182391948817411793)
XLA Ops:
  18.7 23.4 %all-gather.5.cloned.1.call-done = bf16[512,4,768]{2,0,1:T(8,128)(2,1)} async-done(((bf16[128,4,768]{2,0,1:T(8,128)(2,1)}), bf16[512,4,768]{2,0,1:T(8,128)(2,1)}) %all-gather.5.cloned.1.call-update) | async-done | bytes 3145744 | tf_op jit(solution)/shard_map/all_gather | solution.py:63
  46.9 10.6 %fusion.73 = (f32[4,12,128]{2,1,0:T(8,128)S(1)}, f32[4,12,128,512]{3,2,1,0:T(8,128)}) fusion(pred[4,512]{1,0:T(4,128)(4,1)S(1)} %iota_compare_fusion, bf16[128,4,12,64]{0,3,2,1:T(8,128)(2,1)S(1)} %bitcast.113, bf16[512,4,12,64]{0,3,2,1:T(8,128)(2,1)} %bitcast.108), kind=kOutput, calls=%fused_computation.132 | convolution fusion | flops 415236608 | bytes 16541696 | tf_op jit(solution)/shard_map/sub | solution.py:76
  57.5 15.3 %all-gather.3.cloned.1.call-done = bf16[512,4,768]{2,0,1:T(8,128)(2,1)} async-done(((bf16[128,4,768]{2,0,1:T(8,128)(2,1)}), bf16[512,4,768]{2,0,1:T(8,128)(2,1)}) %all-gather.3.cloned.1.call-update) | async-done | bytes 3145744 | tf_op jit(solution)/shard_map/all_gather | solution.py:64
  77.5 7.9 fusion.38
  86.8 7.0 fusion.33
  93.9 14.6 %multiply_convert_fusion.2 = (bf16[128,4,3072]{2,0,1:T(8,128)(2,1)S(1)}, f32[128,4,3072]{2,0,1:T(8,128)S(1)}) fusion(f32[128,4,3072]{2,0,1:T(8,128)S(1)} %get-tuple-element.117, f32[3072]{0:T(1024)S(1)} %convert_element_type.217, u8[128,3072]{1,0:T(8,128)(4,1)S(1)} %get-tuple-element.69, u8[128,3072]{1,0:T(8,128)(4,1)S(1)} %get-tuple-element.68), kind=kLoop, calls=%fused_computation.17 | loop fusion | flops 111673344 | bytes 16527360 | tf_op jit(solution)/shard_map/convert_element_type | solution.py:90
  115.5 9.3 convert_reduce_fusion
  124.8 6.6 multiply_reduce_fusion.1
  137.6 7.0 fusion.25
  144.6 8.8 multiply_reduce_fusion
  158.1 9.3 multiply_convert_fusion
  175.7 5.9 pad_maximum_fusion
  186.1 7.9 convert_reduce_fusion.5
  199.6 40.6 %reduce-scatter.14.cloned.1.call-done = bf16[128,4,1536]{2,0,1:T(8,128)(2,1)} async-done(((bf16[512,4,1536]{2,0,1:T(8,128)(2,1)}), bf16[128,4,1536]{2,0,1:T(8,128)(2,1)}) %reduce-scatter.14.cloned.1.call-update) | async-done | bytes 1572880 | tf_op jit(solution)/shard_map/reduce_scatter | solution.py:128
  253.4 7.2 convolution_bitcast_fusion.1
  261.8 8.2 convolution_bitcast_fusion
  276.1 36.9 %reduce-scatter.16.cloned.1.call-done = f32[96,768]{1,0:T(8,128)} async-done(((f32[768,768]{1,0:T(8,128)}), f32[96,768]{1,0:T(8,128)}) %reduce-scatter.16.cloned.1.call-update) | async-done | bytes 294928 | tf_op jit(solution)/shard_map/reduce_scatter | solution.py:159
  314.7 70.2 %reduce-scatter.22.cloned.1.call-done = f32[96,768]{1,0:T(8,128)} async-done(((f32[768,768]{1,0:T(8,128)}), f32[96,768]{1,0:T(8,128)}) %reduce-scatter.22.cloned.1.call-update) | async-done | bytes 294928
  386.6 70.0 %reduce-scatter.26.cloned.1.call-done = f32[96,768]{1,0:T(8,128)} async-done(((f32[768,768]{1,0:T(8,128)}), f32[96,768]{1,0:T(8,128)}) %reduce-scatter.26.cloned.1.call-update) | async-done | bytes 294928
  458.4 70.1 %reduce-scatter.24.cloned.1.call-done = f32[96,768]{1,0:T(8,128)} async-done(((f32[768,768]{1,0:T(8,128)}), f32[96,768]{1,0:T(8,128)}) %reduce-scatter.24.cloned.1.call-update) | async-done | bytes 294928
  530.4 164.6 %reduce-scatter.18.cloned.1.call-done = f32[96,3072]{1,0:T(8,128)} async-done(((f32[768,3072]{1,0:T(8,128)}), f32[96,3072]{1,0:T(8,128)}) %reduce-scatter.18.cloned.1.call-update) | async-done | bytes 1179664 | tf_op jit(solution)/shard_map/reduce_scatter | solution.py:163
  697.1 164.3 %reduce-scatter.20.cloned.1.call-done = f32[384,768]{1,0:T(8,128)} async-done(((f32[3072,768]{1,0:T(8,128)}), f32[384,768]{1,0:T(8,128)}) %reduce-scatter.20.cloned.1.call-update) | async-done | bytes 1179664 | tf_op jit(solution)/shard_map/reduce_scatter | solution.py:165
  865.0 35.6 %all-reduce.9 = (bf16[768]{0:T(1024)(128)(2,1)S(1)}, bf16[768]{0:T(1024)(128)(2,1)S(1)}, bf16[768]{0:T(1024)(128)(2,1)S(1)}, bf16[768]{0:T(1024)(128)(2,1)S(1)},...) all-reduce(f32[768]{0:T(1024)S(1)} %reduce_sum.216, ...), channel_id=4, replica_groups=mesh['dp'=8,'sp'=4] {'dp'}, use_global_device_ids=true, to_apply=%region_15.16.clone | all-reduce | flops 9216 | bytes 55296
  901.3 6.4 all-reduce.10
  (201 shorter events, 112.4 us)
Async XLA Ops:
  7.2 78.3 %copy-start = (bf16[768,768]{1,0:T(8,128)(2,1)S(1)}, bf16[768,768]{1,0:T(8,128)(2,1)}, u32[]{:S(2)}) copy-start(bf16[768,768]{1,0:T(8,128)(2,1)} %param.25) | copy-start | bytes 3538948
  7.2 34.8 %all-gather.5.cloned.1.call-start = ((), (), s32[]{:S(2)}) async-start(), calls=%async_computation.8 | async-start | bytes 3932160 | tf_op jit(solution)/shard_map/all_gather | solution.py:63
  10.7 62.1 %all-gather.3.cloned.1.call-start = ((), (), s32[]{:S(2)}) async-start(), calls=%async_computation.7 | async-start | bytes 3932160 | tf_op jit(solution)/shard_map/all_gather | solution.py:64
  12.5 227.7 %reduce-scatter.14.cloned.1.call-start = ((), (), s32[]{:S(2)}) async-start(), calls=%async_computation.9 | async-start | bytes 7864320 | tf_op jit(solution)/shard_map/reduce_scatter | solution.py:128
  18.0 28.9 %copy-start.8 = (bf16[128,4,768]{0,2,1:T(8,128)(2,1)}, bf16[128,4,768]{0,2,1:T(8,128)(2,1)S(1)}, u32[]{:S(2)}) copy-start(bf16[128,4,768]{0,2,1:T(8,128)(2,1)S(1)} %copy.93) | copy-start | bytes 2359300
  57.5 20.0 %copy-start.19 = (f32[4,12,128]{2,1,0:T(8,128)}, f32[4,12,128]{2,1,0:T(8,128)S(1)}, u32[]{:S(2)}) copy-start(f32[4,12,128]{2,1,0:T(8,128)S(1)} %get-tuple-element.113) | copy-start | bytes 73732
  86.4 45.0 %copy-start.21 = (f32[128,4]{0,1:T(4,128)}, f32[128,4]{0,1:T(4,128)S(1)}, u32[]{:S(2)}) copy-start(f32[128,4]{0,1:T(4,128)S(1)} %broadcast_multiply_fusion.1) | copy-start | bytes 6148
  86.4 22.1 %slice-start = ((s8[4718592]{0:T(1024)(128)(4,1)}), s8[4194304]{0:T(1024)(128)(4,1)S(1)}, s32[]{:S(2)}) async-start(s8[4718592]{0:T(1024)(128)(4,1)} %bitcast.122), calls=%async_computation.17 | async-start | bytes 8388608
  86.8 44.7 %copy-start.31 = (f32[128,4]{0,1:T(4,128)}, f32[128,4]{0,1:T(4,128)S(1)}, u32[]{:S(2)}) copy-start(f32[128,4]{0,1:T(4,128)S(1)} %fusion.66) | copy-start | bytes 6148
  86.8 21.8 %slice-start.1 = ((s8[4718592]{0:T(1024)(128)(4,1)}), s8[524288]{0:T(1024)(128)(4,1)S(1)}, s32[]{:S(2)}) async-start(s8[4718592]{0:T(1024)(128)(4,1)} %bitcast.122), calls=%async_computation.18 | async-start | bytes 1048576
  93.8 14.7 %copy-start.36 = (f32[768]{0:T(1024)S(1)}, f32[768]{0:T(1024)}, u32[]{:S(2)}) copy-start(f32[768]{0:T(1024)} %convert_element_type.219) | copy-start | bytes 9220
  181.7 131.4 %reduce-scatter.16.cloned.1.call-start = ((), (), s32[]{:S(2)}) async-start(), calls=%async_computation.10 | async-start | bytes 2654208 | tf_op jit(solution)/shard_map/reduce_scatter | solution.py:159
  186.1 198.8 %reduce-scatter.22.cloned.1.call-start = ((), (), s32[]{:S(2)}) async-start(), calls=%async_computation.13 | async-start | bytes 2654208
  199.4 257.2 %reduce-scatter.26.cloned.1.call-start = ((), (), s32[]{:S(2)}) async-start(), calls=%async_computation.15 | async-start | bytes 2654208
  246.7 281.9 %reduce-scatter.24.cloned.1.call-start = ((), (), s32[]{:S(2)}) async-start(), calls=%async_computation.14 | async-start | bytes 2654208
  253.3 441.6 %reduce-scatter.18.cloned.1.call-start = ((), (), s32[]{:S(2)}) async-start(), calls=%async_computation.11 | async-start | bytes 10616832 | tf_op jit(solution)/shard_map/reduce_scatter | solution.py:163
  260.7 600.7 %reduce-scatter.20.cloned.1.call-start = ((), (), s32[]{:S(2)}) async-start(), calls=%async_computation.12 | async-start | bytes 10616832 | tf_op jit(solution)/shard_map/reduce_scatter | solution.py:165
  270.0 649.2 %all-reduce.14.cloned.1.call-start = ((), (), s32[]{:S(2)}) async-start(), calls=%async_computation.16 | async-start | bytes 3833856 | tf_op jit(solution)/shard_map/psum | solution.py:172
  530.3 334.6 %copy-start.25 = (f32[768]{0:T(1024)S(1)}, f32[768]{0:T(1024)}, u32[]{:S(2)}) copy-start(f32[768]{0:T(1024)} %get-tuple-element.72) | copy-start | bytes 9220
  530.3 334.6 %copy-start.26 = (f32[768]{0:T(1024)S(1)}, f32[768]{0:T(1024)}, u32[]{:S(2)}) copy-start(f32[768]{0:T(1024)} %get-tuple-element.77) | copy-start | bytes 9220
  530.4 334.6 %copy-start.27 = (f32[768]{0:T(1024)S(1)}, f32[768]{0:T(1024)}, u32[]{:S(2)}) copy-start(f32[768]{0:T(1024)} %get-tuple-element.102) | copy-start | bytes 9220
  530.4 334.6 %copy-start.30 = (f32[3072]{0:T(1024)S(1)}, f32[3072]{0:T(1024)}, u32[]{:S(2)}) copy-start(f32[3072]{0:T(1024)} %get-tuple-element.125) | copy-start | bytes 36868
  863.5 51.1 %copy-start.4 = (f32[128,4,768]{2,0,1:T(8,128)S(1)}, f32[128,4,768]{2,0,1:T(8,128)}, u32[]{:S(2)}) copy-start(f32[128,4,768]{2,0,1:T(8,128)} %copy-done.3) | copy-start | bytes 4718596
  914.7 14.8 %copy-start.1 = (bf16[768,768]{1,0:T(8,128)(2,1)S(1)}, bf16[768,768]{1,0:T(8,128)(2,1)}, u32[]{:S(2)}) copy-start(bf16[768,768]{1,0:T(8,128)(2,1)} %param.25) | copy-start | bytes 3538948
  (35 other events, 133.7 us)
Sparse Core Ops, SparseCore 0:
  10.8 31.2 all-gather.4
  44.2 28.5 all-gather.2
  181.8 58.3 reduce-scatter.13
  244.0 69.0 reduce-scatter.15
  316.8 68.0 reduce-scatter.21
  388.6 68.0 reduce-scatter.25
  460.6 67.9 reduce-scatter.23
  532.6 162.3 reduce-scatter.17
  699.0 162.3 reduce-scatter.19
  865.4 48.9 all-reduce.13
where the time goes:
time: 941 us; the launch traced here: 937 us
  waiting for transfers between devices  656 us (70%)
  matrix products  116 us (12%)
  other arithmetic  55.8 us (6%)
  local copies, waits for them, and re-layouts  50.7 us (5%)
  blocking collectives  42 us (4%)
  between operations  16.3 us (2%)
    unnamed x13, waiting for transfers between devices  211 us
    reduce_scatter x1, waiting for transfers between devices, shards(): lax.psum_scatter(grad_up, 'dp', scatter_dimension=0, tiled=True)  165 us
    reduce_scatter x1, waiting for transfers between devices, shards(): lax.psum_scatter(grad_down, 'dp', scatter_dimension=0, tiled=True)  164 us
    reduce_scatter x1, waiting for transfers between devices, shards(): lax.psum_scatter(jnp.concatenate((key_part.reshape(row_count, pair_count,...  40.6 us
    reduce_scatter x1, waiting for transfers between devices, shards(): lax.psum_scatter(grad_out, 'dp', scatter_dimension=0, tiled=True)  36.9 us
    unnamed x1, blocking collectives  35.6 us
    unnamed x119, local copies, waits for them, and re-layouts  29.8 us
    dot_general x6, matrix products, weight_grad(): jnp.einsum('spd,spe->de', left, right, preferred_element_type=jnp.float32)  27.6 us
  transfers between devices with their start and end apart: 10, of which 9 were waited for; matrix products, arithmetic and copies ran while one was open for 10% of the time, Pallas kernels for 0%

commit v1 on v0

--- a/solution.py
+++ b/solution.py
@@ -1,10 +1,670 @@
+import functools
+
 import jax
 import jax.numpy as jnp
 from jax import lax
+from jax.experimental import pallas as pl
+from jax.experimental.pallas import tpu as pltpu
 from jax.sharding import PartitionSpec as P
 
 HEADS = 12
 HD = 64
+EPS = 1e-05
+MESH_ID = pl.DeviceIdType.MESH
+BF = jnp.bfloat16
+F32 = jnp.float32
+
+
+def nn(left, right):
+    return jnp.dot(left, right, preferred_element_type=F32)
+
+
+def nt(left, right):
+    return lax.dot_general(left, right, (((1,), (1,)), ((), ())), preferred_element_type=F32)
+
+
+def tn(left, right):
+    return lax.dot_general(left, right, (((0,), (0,)), ((), ())), preferred_element_type=F32)
+
+
+def aligned(start, step=128):
+    return pl.multiple_of(start, step)
+
+
+ROUTES = {
+    "A": ("c", "0", "1", "2", "Y"),
+    "B": ("c", "y", "0", "1", "2"),
+    "C": ("c", "1", "2", "0", "Y"),
+}
+UNITS = (
+    ("d", 0), ("d", 1), ("d", 2), ("u", 0), ("u", 1), ("u", 2),
+    ("a", 3), ("a", 0), ("a", 1), ("a", 2),
+)
+PATH = ("A", "B", "A", "C", "B", "A", "B", "A", "B", "A")
+ROWS_VEC = 16
+STAGES = 7
+
+
+def land_shape(rows, cols, route, stage):
+    lead, r, c = [2, 2, 2], rows, cols
+    for kind in ROUTES[route][: stage + 1]:
+        if kind == "c":
+            c //= 2
+        elif kind == "y":
+            r //= 2
+        elif kind != "Y":
+            lead[2 - int(kind)] = 0
+    return tuple(n for n in lead if n) + (r, c)
+
+
+def layer_kernel(*refs):
+    it = iter(refs)
+    (len_ref, vec_ref, tok_ref, cot_ref, wq_ref, wk_ref, wv_ref, wo_ref, wu_ref, wd_ref) = (next(it) for _ in range(10))
+    (mix_out, dtok_out, ga_out, gu_out, gd_out, gv_out) = (next(it) for _ in range(6))
+    (x_s, cot_s, wa, wu, wd, q_s, k_s, v_s, p_s, att_s, linv_s, xh_s, rs_s, hl_s, act_s, gp_s, acc_s, dh_s, mix_s) = (
+        next(it) for _ in range(19)
+    )
+    vs, vl = next(it), next(it)
+    lands = [[next(it) for _ in ROUTES[path]] for path in PATH]
+    finals = [next(it) if path != "B" else None for path in PATH]
+    (wsem, lsem, asend, arecv, usend, urecv, vsend, vrecv) = (next(it) for _ in range(8))
+
+    rows_loc, width = tok_ref.shape[1], tok_ref.shape[2]
+    total = rows_loc * 4
+    half = total // 2
+    dp, sp = lax.axis_index("dp"), lax.axis_index("sp")
+    bits = [lax.rem(lax.div(dp, 2**k), 2) for k in range(3)]
+    core, ybit = lax.rem(sp, 2), lax.div(sp, 2)
+
+    def sp_xor(k):
+        low, high = core, ybit
+        if k & 1:
+            low = 1 - low
+        if k & 2:
+            high = 1 - high
+        return high * 2 + low
+
+    def peer(kind):
+        if kind == "c":
+            return (dp, sp_xor(1))
+        if kind in "yY":
+            return (dp, sp_xor(2))
+        k = int(kind)
+        return (dp + 2**k * (1 - 2 * bits[k]), sp)
+
+    barrier = pltpu.get_barrier_semaphore()
+    greet = [(dp, sp_xor(k)) for k in (1, 2, 3)] + [peer(k) for k in "012"]
+    for other in greet:
+        pl.semaphore_signal(barrier, inc=1, device_id=other, device_id_type=MESH_ID)
+
+    loads = []
+
+    def load(src, dst):
+        copy = pltpu.make_async_copy(src, dst, wsem.at[len(loads)])
+        copy.start()
+        loads.append(copy)
+        return copy
+
+    own_tok = load(tok_ref.at[sp], x_s.at[pl.ds(aligned(sp * rows_loc), rows_loc)])
+    attn_loads = [load(ref, wa.at[i]) for i, ref in enumerate((wq_ref, wk_ref, wv_ref, wo_ref))]
+    pl.semaphore_wait(barrier, len(greet))
+
+    def exchange(src, dst, base):
+        copies = []
+        for k in (2, 3, 1):
+            other = sp_xor(k)
+            copy = pltpu.make_async_remote_copy(
+                src_ref=src.at[other],
+                dst_ref=dst.at[pl.ds(aligned(sp * rows_loc), rows_loc)],
+                send_sem=asend.at[base + k - 1],
+                recv_sem=arecv.at[base + k - 1],
+                device_id=(dp, other),
+                device_id_type=MESH_ID,
+            )
+            copy.start()
+            copies.append(copy)
+        return copies
+
+    tok_copies = exchange(tok_ref, x_s, 0)
+    up_loads = [
+        [load(wu_ref.at[:, :, :, :, pl.ds(384 * r + 128 * j, 128)], wu.at[j, :, :, :, :, pl.ds(128 * r, 128)]) for r in range(8)]
+        for j in range(3)
+    ]
+    down_loads = [load(wd_ref.at[:, :, :, j], wd.at[j]) for j in range(3)]
+    own_cot = load(cot_ref.at[sp], cot_s.at[pl.ds(aligned(sp * rows_loc), rows_loc)])
+
+    state = [dict(stage=0, copies=[]) for _ in UNITS]
+
+    def home(unit):
+        kind, j = unit
+        return {"d": wd, "u": wu, "a": wa}[kind], j
+
+    def region(unit, kinds, last_other=False):
+        ref, j = home(unit)
+        rows, cols = ref.shape[4], ref.shape[5]
+        lead = [slice(None)] * 3
+        rsl, csl = slice(None), slice(None)
+        for i, kind in enumerate(kinds):
+            flip = last_other and i == len(kinds) - 1
+            if kind == "c":
+                at = 1 - core if flip else core
+                csl = pl.ds(aligned(at * (cols // 2)), cols // 2)
+            elif kind == "y":
+                at = 1 - ybit if flip else ybit
+                rsl = pl.ds(aligned(at * (rows // 2), 16), rows // 2)
+            elif kind != "Y":
+                b = bits[int(kind)]
+                lead[2 - int(kind)] = 1 - b if flip else b
+        return ref, (j, *lead, rsl, csl)
+
+    def send(n, stage, src, dst, to):
+        copy = pltpu.make_async_remote_copy(
+            src_ref=src,
+            dst_ref=dst,
+            send_sem=usend.at[n, stage],
+            recv_sem=urecv.at[n, stage],
+            device_id=to,
+            device_id_type=MESH_ID,
+        )
+        copy.start()
+        state[n]["copies"].append(copy)
+
+    def out_region(unit, at_core, at_y=None):
+        kind, j = unit
+        ref = {"d": gd_out, "u": gu_out, "a": ga_out}[kind]
+        rows, cols = ref.shape[1], ref.shape[2]
+        rsl = slice(None) if at_y is None else pl.ds(aligned(at_y * (rows // 2), 16), rows // 2)
+        return ref.at[j, rsl, pl.ds(aligned(at_core * (cols // 2)), cols // 2)]
+
+    def advance(n):
+        unit, path = UNITS[n], PATH[n]
+        route = ROUTES[path]
+        stage = state[n]["stage"]
+        state[n]["stage"] += 1
+        if stage > 0:
+            state[n]["copies"][stage - 1].wait_recv()
+            kind = route[stage - 1]
+            ref, at = region(unit, route[:stage])
+            if kind == "Y":
+                finals[n][...] = ref[at] + lands[n][stage - 1][...]
+            else:
+                ref[at] = ref[at] + lands[n][stage - 1][...]
+        if stage < len(route):
+            kind = route[stage]
+            ref, at = region(unit, route[: stage + 1], last_other=True)
+            send(n, stage, ref.at[at], lands[n][stage], peer(kind))
+            return
+        if path == "B":
+            ref, at = region(unit, route)
+            src, dst = ref.at[at], out_region(unit, core, ybit)
+            for k in (1, 2, 3):
+                send(n, stage + k - 1, src, dst, (dp, sp_xor(k)))
+        else:
+            src, dst = finals[n], out_region(unit, core)
+            send(n, stage, src, dst, peer("c"))
+        local = pltpu.make_async_copy(src, dst, lsem.at[n])
+        local.start()
+        state[n]["local"] = local
+
+    def finish(n):
+        while state[n]["stage"] <= len(ROUTES[PATH[n]]):
+            advance(n)
+        for copy in state[n]["copies"][len(ROUTES[PATH[n]]) :]:
+            copy.wait_recv()
+        for copy in state[n]["copies"]:
+            copy.wait_send()
+        state[n]["local"].wait()
+
+    def vec(row, size=None):
+        return vec_ref[pl.ds(row, 1), pl.ds(0, width if size is None else size)]
+
+    def put_vec(row, value):
+        vs[0, pl.ds(row, 1), pl.ds(0, value.shape[1])] = value
+
+    vs[0] = jnp.zeros(vs.shape[1:], F32)
+
+    def qkv(start):
+        x = x_s[pl.ds(start, half), :]
+
+        def tile(i, carry):
+            cols = pl.ds(aligned(i * 256), 256)
+            for w, (dst, row) in enumerate(((q_s, 0), (k_s, None), (v_s, 1))):
+                r = nn(x, wa[w, :, :, :, :, cols].reshape(width, 256))
+                if row is not None:
+                    r = r + vec_ref[pl.ds(row, 1), cols]
+                if w == 0:
+                    r = r * HD ** (-0.5)
+                dst[pl.ds(start, half), cols] = r.astype(BF)
+            return carry
+
+        lax.fori_loop(0, width // 256, tile, 0)
+
+    for copy in attn_loads[:3]:
+        copy.wait()
+    own_tok.wait()
+    tok_copies[2].wait_recv()
+    qkv(aligned(ybit * half))
+    tok_copies[0].wait_recv()
+    tok_copies[1].wait_recv()
+    cot_copies = exchange(cot_ref, cot_s, 3)
+    qkv(aligned((1 - ybit) * half))
+
+    length = len_ref[sp]
+    lane = lax.broadcasted_iota(jnp.int32, (total, 128), 1)
+    low = lane < HD
+    groups = HEADS // 2
+
+    def attend(g, carry):
+        cols = pl.ds(aligned(g * 128), 128)
+        q2, k2, v2 = q_s[:, cols], k_s[:, cols], v_s[:, cols]
+        outs = []
+        for h in range(2):
+            mine = low if h == 0 else jnp.logical_not(low)
+            qh = jnp.where(mine, q2, jnp.zeros_like(q2))
+            vh = jnp.where(mine, v2, jnp.ones_like(v2))
+            s = nt(qh, k2)
+            s = jnp.where(lax.broadcasted_iota(jnp.int32, s.shape, 1) < length, s, -1e30)
+            e = jnp.exp(s - jnp.max(s, axis=-1, keepdims=True)).astype(BF)
+            p_s[g * 2 + h] = e
+            outs.append(nn(e, vh))
+        num = jnp.where(low, outs[0], outs[1])
+        den = pltpu.roll(jnp.where(low, outs[1], outs[0]), HD, axis=1)
+        inv = 1.0 / den
+        linv_s[:, cols] = inv.astype(BF)
+        att_s[:, cols] = (num * inv).astype(BF)
+        return carry
+
+    lax.fori_loop(0, groups, attend, 0)
+
+    attn_loads[3].wait()
+    wo = wa.at[3]
+
+    def first_norm(i, carry):
+        rows = pl.ds(aligned(i * 256, 256), 256)
+        r = nn(att_s[rows, :], wo[...].reshape(width, width)) + vec(2) + x_s[rows, :].astype(F32)
+        mean = jnp.mean(r, axis=-1, keepdims=True)
+        center = r - mean
+        rs = lax.rsqrt(jnp.mean(center * center, axis=-1, keepdims=True) + EPS)
+        xh = center * rs
+        hidden = xh * vec(3) + vec(4)
+        rs_s[rows, :] = rs
+        xh_s[rows, :] = xh
+        acc_s[rows, :] = hidden
+        hl_s[rows, :] = hidden.astype(BF)
+        return carry
+
+    lax.fori_loop(0, total // 256, first_norm, 0)
+
+    for j in range(3):
+        for copy in up_loads[j]:
+            copy.wait()
+
+        def up(t, carry, j=j):
+            cols = pl.ds(aligned(t * 256), 256)
+            inner = nn(hl_s[...], wu[j, :, :, :, :, cols].reshape(width, 256)) + vec_ref[pl.ds(10 + j, 1), cols]
+            cdf = 0.5 + 0.5 * lax.erf(inner * (0.5**0.5))
+            pdf = jnp.exp(-0.5 * inner * inner) * 0.3989422804014327
+            act_s[j, :, cols] = (inner * cdf).astype(BF)
+            gp_s[j, :, cols] = (cdf + inner * pdf).astype(BF)
+            return carry
+
+        lax.fori_loop(0, 4, up, 0)
+
+    for copy in down_loads:
+        copy.wait()
+
+    def down(i, carry):
+        cols = pl.ds(aligned(i * 256), 256)
+        r = acc_s[:, cols] + vec_ref[pl.ds(5, 1), cols]
+        for j in range(3):
+            r = r + nn(act_s[j], wd[j, :, :, :, :, cols].reshape(1024, 256))
+        acc_s[:, cols] = r
+        return carry
+
+    lax.fori_loop(0, width // 256, down, 0)
+
+    own_cot.wait()
+    for copy in cot_copies:
+        copy.wait_recv()
+
+    def second_norm(i, carry):
+        rows = pl.ds(aligned(i * 128, 128), 128)
+        r = acc_s[rows, :]
+        mean = jnp.mean(r, axis=-1, keepdims=True)
+        center = r - mean
+        rs = lax.rsqrt(jnp.mean(center * center, axis=-1, keepdims=True) + EPS)
+        xh = center * rs
+        mix_s[rows, :] = (xh * vec(6) + vec(7)).astype(BF)
+        dy = cot_s[rows, :].astype(F32)
+        dxh = dy * vec(6)
+        d2 = rs * (dxh - jnp.mean(dxh, axis=-1, keepdims=True) - xh * jnp.mean(dxh * xh, axis=-1, keepdims=True))
+        acc_s[rows, :] = d2
+        low2 = d2.astype(BF)
+        cot_s[rows, :] = low2
+        sums = (
+            jnp.sum(dy * xh, axis=0, keepdims=True),
+            jnp.sum(dy, axis=0, keepdims=True),
+            jnp.sum(low2.astype(F32), axis=0, keepdims=True),
+        )
+        return tuple(c + s for c, s in zip(carry, sums))
+
+    zero = jnp.zeros((1, width), F32)
+    g_gain, g_shift, g_bdown = lax.fori_loop(0, total // 128, second_norm, (zero, zero, zero))
+    put_vec(6, g_gain)
+    put_vec(7, g_shift)
+    put_vec(5, g_bdown)
+
+    def give_back(src, dst, base):
+        copies = []
+        for k in (2, 3, 1):
+            other = sp_xor(k)
+            copy = pltpu.make_async_remote_copy(
+                src_ref=src.at[pl.ds(aligned(other * rows_loc), rows_loc)],
+                dst_ref=dst.at[sp],
+                send_sem=asend.at[base + k - 1],
+                recv_sem=arecv.at[base + k - 1],
+                device_id=(dp, other),
+                device_id_type=MESH_ID,
+            )
+            copy.start()
+            copies.append(copy)
+        own = pltpu.make_async_copy(src.at[pl.ds(aligned(sp * rows_loc), rows_loc)], dst.at[sp], lsem.at[10 + base // 3])
+        own.start()
+        return copies, own
+
+    mix_copies, mix_own = give_back(mix_s, mix_out, 6)
+
+    def inner_back(j):
+        def tile(i, carry):
+            a, b = lax.div(i, 2), lax.rem(i, 2)
+            cols = pl.ds(aligned(i * 256), 256)
+            d = nt(cot_s[...], wd[j, a, b].reshape(256, width)) * gp_s[j, :, cols].astype(F32)
+            d = d.astype(BF)
+            gp_s[j, :, cols] = d
+            vs[0, pl.ds(10 + j, 1), cols] = jnp.sum(d.astype(F32), axis=0, keepdims=True)
+            return carry
+
+        lax.fori_loop(0, 4, tile, 0)
+
+    def grad_down(j):
+        def tile(i, carry):
+            a, b = lax.div(i, 2), lax.rem(i, 2)
+            cols = pl.ds(aligned(i * 256), 256)
+            wd[j, a, b] = tn(act_s[j, :, cols], cot_s[...]).astype(BF).reshape(2, 128, width)
+            return carry
+
+        lax.fori_loop(0, 4, tile, 0)
+
+    def hidden_back(j):
+        def tile(a, carry):
+            cols = pl.ds(aligned(a * 384), 384)
+            acc_s[:, cols] += nt(gp_s[j], wu[j, a].reshape(384, 1024))
+            return carry
+
+        lax.fori_loop(0, 2, tile, 0)
+
+    def grad_up(j):
+        def tile(i, carry):
+            a, b = lax.div(i, 4), lax.rem(i, 4)
+            cols = pl.ds(aligned(b * 256), 256)
+            r = tn(hl_s[:, pl.ds(aligned(a * 384), 384)], gp_s[j, :, cols])
+            wu[j, a, :, :, :, cols] = r.astype(BF).reshape(2, 2, 96, 256)
+            return carry
+
+        lax.fori_loop(0, 8, tile, 0)
+
+    inner_back(0)
+    grad_down(0)
+    advance(0)
+    inner_back(1)
+    grad_down(1)
+    advance(1)
+    advance(0)
+    inner_back(2)
+    grad_down(2)
+    advance(2)
+    advance(1)
+    hidden_back(0)
+    grad_up(0)
+    advance(3)
+    advance(2)
+    hidden_back(1)
+    advance(0)
+    advance(3)
+    grad_up(1)
+    advance(4)
+    hidden_back(2)
+    advance(1)
+    advance(4)
+    grad_up(2)
+    advance(5)
+
+    def first_back(i, carry):
+        rows = pl.ds(aligned(i * 128, 128), 128)
+        dy = acc_s[rows, :]
+        xh = xh_s[rows, :]
+        dxh = dy * vec(3)
+        d1 = rs_s[rows, :] * (
+            dxh - jnp.mean(dxh, axis=-1, keepdims=True) - xh * jnp.mean(dxh * xh, axis=-1, keepdims=True)
+        )
+        acc_s[rows, :] = d1
+        low1 = d1.astype(BF)
+        dh_s[rows, :] = low1
+        sums = (
+            jnp.sum(dy * xh, axis=0, keepdims=True),
+            jnp.sum(dy, axis=0, keepdims=True),
+            jnp.sum(low1.astype(F32), axis=0, keepdims=True),
+        )
+        return tuple(c + s for c, s in zip(carry, sums))
+
+    g_gain, g_shift, g_bout = lax.fori_loop(0, total // 128, first_back, (zero, zero, zero))
+    put_vec(3, g_gain)
+    put_vec(4, g_shift)
+    put_vec(2, g_bout)
+    advance(5)
+    advance(0)
+    advance(2)
+
+    def attended_back(a, carry):
+        cols = pl.ds(aligned(a * 384), 384)
+        d = nt(dh_s[...], wo[a].reshape(384, width)) * linv_s[:, cols].astype(F32)
+        mix2[:, cols] = d.astype(BF)
+        return carry
+
+    mix2 = hl_s
+    lax.fori_loop(0, 2, attended_back, 0)
+
+    def grad_out(i, carry):
+        a, b = lax.div(i, 3), lax.rem(i, 3)
+        cols = pl.ds(aligned(b * 256), 256)
+        r = tn(att_s[:, pl.ds(aligned(a * 384), 384)], dh_s[:, cols])
+        wa[3, a, :, :, :, cols] = r.astype(BF).reshape(2, 2, 96, 256)
+        return carry
+
+    lax.fori_loop(0, 6, grad_out, 0)
+    advance(6)
+    advance(3)
+    advance(1)
+    advance(0)
+
+    def attend_back(g, carry):
+        cols = pl.ds(aligned(g * 128), 128)
+        q2, k2, v2, d2 = q_s[:, cols], k_s[:, cols], v_s[:, cols], mix2[:, cols]
+        prod = d2.astype(F32) * att_s[:, cols].astype(F32)
+        dqs, dks, dvs = [], [], []
+        for h in range(2):
+            mine = low if h == 0 else jnp.logical_not(low)
+            dah = jnp.where(mine, d2, jnp.zeros_like(d2))
+            delta = jnp.sum(jnp.where(mine, prod, 0.0), axis=-1, keepdims=True)
+            e = p_s[g * 2 + h]
+            ds = (e.astype(F32) * (nt(dah, v2) - delta)).astype(BF)
+            dqs.append(nn(ds, k2))
+            dks.append(tn(ds, q2))
+            dvs.append(tn(e, d2))
+        dq = (jnp.where(low, dqs[0], dqs[1]) * HD ** (-0.5)).astype(BF)
+        dk = jnp.where(low, dks[0], dks[1]).astype(BF)
+        dv = jnp.where(low, dvs[0], dvs[1]).astype(BF)
+        q_s[:, cols] = dq
+        k_s[:, cols] = dk
+        v_s[:, cols] = dv
+        vs[0, pl.ds(0, 1), cols] = jnp.sum(dq.astype(F32), axis=0, keepdims=True)
+        vs[0, pl.ds(1, 1), cols] = jnp.sum(dv.astype(F32), axis=0, keepdims=True)
+        return carry
+
+    lax.fori_loop(0, 2, attend_back, 0)
+    for n in (6, 5, 4, 2, 1, 3):
+        advance(n)
+    lax.fori_loop(2, 4, attend_back, 0)
+    for n in (0, 4, 5, 6, 3, 2, 1):
+        advance(n)
+    lax.fori_loop(4, 6, attend_back, 0)
+
+    vec_copies = []
+
+    def vec_step(i):
+        if i > 0:
+            vec_copies[i - 1].wait_recv()
+            vs[i] = vs[i - 1] + vl[i - 1]
+        if i < 5:
+            copy = pltpu.make_async_remote_copy(
+                src_ref=vs.at[i],
+                dst_ref=vl.at[i],
+                send_sem=vsend.at[i],
+                recv_sem=vrecv.at[i],
+                device_id=peer("c012y"[i]),
+                device_id_type=MESH_ID,
+            )
+            copy.start()
+            vec_copies.append(copy)
+
+    vec_step(0)
+
+    def tokens_back(w, src):
+        def tile(a, carry):
+            cols = pl.ds(aligned(a * 384), 384)
+            r = acc_s[:, cols] + nt(src[...], wa[w, a].reshape(384, width))
+            if w == 2:
+                dh_s[:, cols] = r.astype(BF)
+            else:
+                acc_s[:, cols] = r
+            return carry
+
+        lax.fori_loop(0, 2, tile, 0)
+
+    def grad_proj(w, src):
+        def tile(i, carry):
+            a, b = lax.div(i, 3), lax.rem(i, 3)
+            cols = pl.ds(aligned(b * 256), 256)
+            r = tn(x_s[:, pl.ds(aligned(a * 384), 384)], src[:, cols])
+            wa[w, a, :, :, :, cols] = r.astype(BF).reshape(2, 2, 96, 256)
+            return carry
+
+        lax.fori_loop(0, 6, tile, 0)
+
+    tokens_back(0, q_s)
+    grad_proj(0, q_s)
+    advance(7)
+    vec_step(1)
+    tokens_back(1, k_s)
+    grad_proj(1, k_s)
+    advance(8)
+    advance(7)
+    vec_step(2)
+    tokens_back(2, v_s)
+    grad_proj(2, v_s)
+    advance(9)
+    tok_back, tok_own = give_back(dh_s, dtok_out, 9)
+    advance(8)
+    vec_step(3)
+    advance(9)
+
+    for _ in range(4):
+        for n in range(len(UNITS)):
+            if state[n]["stage"] <= len(ROUTES[PATH[n]]):
+                advance(n)
+        if len(vec_copies) < 5:
+            vec_step(len(vec_copies))
+    vec_step(5)
+    gv_out[...] = vs[5]
+    for n in range(len(UNITS)):
+        finish(n)
+    for copy in vec_copies:
+        copy.wait_send()
+    for copy in tok_copies + cot_copies:
+        copy.wait_send()
+    for copy in mix_copies + tok_back:
+        copy.wait()
+    mix_own.wait()
+    tok_own.wait()
+
+
+def fused(
+    tokens, lengths, w_query, b_query, w_key, w_value, b_value, w_out, b_out, gain_attn, shift_attn,
+    w_up, b_up, w_down, b_down, gain_ffn, shift_ffn, cotangent,
+):
+    rows_loc, pairs, width = tokens.shape
+    total = rows_loc * 4
+    rows = width // 8
+    rows8 = [b_query, b_value, b_out, gain_attn, shift_attn, b_down, gain_ffn, shift_ffn]
+    table = jnp.stack([jnp.pad(v.astype(F32), (0, 1024 - width)) for v in rows8] + [jnp.zeros((1024,), F32)] * 2)
+    up_bias = b_up.astype(F32).reshape(8, 3, 128).transpose(1, 0, 2).reshape(3, 1024)
+    table = jnp.concatenate([table, up_bias, jnp.zeros((3, 1024), F32)])
+    square = lambda w: w.reshape(2, 2, 2, rows, w.shape[1])
+    args = (
+        lengths, table, tokens.transpose(1, 0, 2), cotangent.transpose(1, 0, 2),
+        square(w_query), square(w_key), square(w_value), square(w_out), square(w_up),
+        w_down.reshape(2, 2, 2, 3, 128, width),
+    )
+    shapes = {"d": (128, width), "u": (rows, 1024), "a": (rows, width)}
+    vm = lambda shape, dtype=BF: pltpu.VMEM(shape, dtype)
+    scratch = [
+        vm((total, width)), vm((total, width)),
+        vm((4, 2, 2, 2, rows, width)), vm((3, 2, 2, 2, rows, 1024)), vm((3, 2, 2, 2, 128, width)),
+        vm((total, width)), vm((total, width)), vm((total, width)),
+        vm((HEADS, total, total)), vm((total, width)), vm((total, width)),
+        vm((total, width), F32), vm((total, 1), F32), vm((total, width)),
+        vm((3, total, 1024)), vm((3, total, 1024)),
+        vm((total, width), F32), vm((total, width)), vm((total, width)),
+        vm((6, ROWS_VEC, 1024), F32), vm((5, ROWS_VEC, 1024), F32),
+    ]
+    for unit, path in zip(UNITS, PATH):
+        scratch += [vm(land_shape(*shapes[unit[0]], path, s)) for s in range(5)]
+    for unit, path in zip(UNITS, PATH):
+        if path != "B":
+            r, c = shapes[unit[0]]
+            scratch.append(vm((r, c // 2)))
+    dma = pltpu.SemaphoreType.DMA
+    scratch += [dma((40,)), dma((14,)), dma((12,)), dma((12,)), dma((10, 8)), dma((10, 8)), dma((5,)), dma((5,))]
+    anywhere = pl.BlockSpec(memory_space=pl.ANY)
+    out = pl.pallas_call(
+        layer_kernel,
+        out_shape=(
+            jax.ShapeDtypeStruct((4, rows_loc, width), BF),
+            jax.ShapeDtypeStruct((4, rows_loc, width), BF),
+            jax.ShapeDtypeStruct((4, rows, width), BF),
+            jax.ShapeDtypeStruct((3, rows, 1024), BF),
+            jax.ShapeDtypeStruct((3, 128, width), BF),
+            jax.ShapeDtypeStruct((ROWS_VEC, 1024), F32),
+        ),
+        in_specs=[pl.BlockSpec(memory_space=pltpu.SMEM), pl.BlockSpec(memory_space=pltpu.VMEM)] + [anywhere] * 8,
+        out_specs=(anywhere,) * 5 + (pl.BlockSpec(memory_space=pltpu.VMEM),),
+        scratch_shapes=scratch,
+        compiler_params=pltpu.CompilerParams(collective_id=0, has_side_effects=True, vmem_limit_bytes=63 * 2**20),
+    )(*args)
+    mixed, dtok, ga, gu, gd, gv = out
+    at = lax.axis_index("dp")
+    low = lax.dynamic_slice(gv[:8, :width].reshape(8, 8, rows), (0, at, 0), (8, 1, rows))[:, 0]
+    bup = lax.dynamic_slice(gv[10:13].reshape(3, 8, 128), (0, at, 0), (3, 1, 128)).reshape(384)
+    ga = ga.astype(F32)
+    return (
+        mixed.transpose(1, 0, 2),
+        dtok.transpose(1, 0, 2),
+        ga[0], low[0], ga[1], ga[2], low[1], ga[3], low[2], low[3], low[4],
+        gu.astype(F32).reshape(3, rows, 8, 128).transpose(1, 2, 0, 3).reshape(rows, 3072),
+        bup,
+        gd.astype(F32).reshape(384, width),
+        low[5], low[6], low[7],
+    )
 
 
 def norm_layer(resid, gain, shift):
@@ -228,8 +888,9 @@
         P(),
         P("sp", "dp", None),
     )
+    fits = mesh.shape["dp"] == 8 and mesh.shape["sp"] == 4
     return jax.shard_map(
-        shards,
+        fused if fits else shards,
         mesh=mesh,
         in_specs=placed,
         out_specs=(

time: 941 us -> 161 us (0.17)
  waiting for transfers between devices: 656 us -> 0 us
  Pallas kernels: 0 us -> 139 us
  matrix products: 116 us -> 0 us
  other arithmetic: 55.8 us -> 6.69 us
  blocking collectives: 42 us -> 0 us
  local copies, waits for them, and re-layouts: 50.7 us -> 14 us
  between operations: 16.3 us -> 0.75 us
    reduce_scatter x4 -> x0, waiting for transfers between devices: 406 us -> none  [the longest x1 165 us: shards(): lax.psum_scatter(grad_up, 'dp', scatter_dimension=0, tiled=True)]
    unnamed x13 -> x0, waiting for transfers between devices: 211 us -> none
    pallas_call x0 -> x1, Pallas kernels: none -> 139 us  [fused(): pl.pallas_call(layer_kernel, out_shape=(jax.ShapeDtypeStruct((4, rows_loc...]
    dot_general x23 -> x0, matrix products: 105 us -> none  [the longest x6 27.6 us: weight_grad(): jnp.einsum('spd,spe->de', left, right, preferred_element_type=jnp.float32)]
    convert_element_type x26 -> x1, other arithmetic: 42.4 us -> 0.09 us  [fused(): ga = ga.astype(F32)]
    all_gather x2 -> x0, waiting for transfers between devices: 38.6 us -> none  [the longest x1 23.4 us: shards(): lax.all_gather(keys_local, 'sp', axis=0, tiled=True)]
    unnamed x1 -> x0, blocking collectives: 35.6 us -> none
    unnamed x119 -> x15, local copies, waits for them, and re-layouts: 29.8 us -> 4.7 us
  transfers between devices with their start and end apart: 10 -> 0, of which waited for: 9 -> 0; matrix products, arithmetic and copies ran while one was open for 10% -> 0% of each run, Pallas kernels for 0% -> 0%
where the time goes in v1:
time: 161 us
  Pallas kernels  139 us (86%)
  local copies, waits for them, and re-layouts  14 us (9%)
  other arithmetic  6.69 us (4%)
    pallas_call x1, Pallas kernels, fused(): pl.pallas_call(layer_kernel, out_shape=(jax.ShapeDtypeStruct((4, rows_loc...  139 us
    another operation x8, other arithmetic, fused(): jnp.stack([jnp.pad(v.astype(F32), (0, 1024 - width)) for v in rows8] + [j...  5.47 us
    unnamed x15, local copies, waits for them, and re-layouts  4.7 us

profile of v1, /device:TPU:0, one launch (start us, length us, event | category | flops | bytes accessed | tf_op | source)
XLA Modules:
  0.0 160.6 jit_solution(10076569567421827022)
XLA Ops:
  0.7 0.7 pad_convert_fusion.7
  1.3 0.7 pad_convert_fusion.6
  2.0 0.7 pad_convert_fusion.5
  2.7 0.7 pad_convert_fusion.4
  3.4 0.7 pad_convert_fusion.3
  4.1 0.7 pad_convert_fusion.2
  4.8 0.7 pad_convert_fusion.1
  5.4 0.7 pad_convert_fusion
  6.1 0.7 reshape.137
  6.8 1.3 concatenate.7.refs_1_
  8.2 2.7 %copy_bitcast_fusion.1 = (bf16[4,128,768]{2,1,0:T(8,128)(2,1)}, bf16[4,128,768]{2,1,0:T(8,128)(2,1)}) fusion(bf16[128,4,768]{2,1,0:T(4,128)(2,1)} %param.35, bf16[128,4,768]{2,1,0:T(4,128)(2,1)} %param.18), kind=kLoop, calls=%fused_computation.1 | loop fusion | bytes 3145728 | tf_op jit(solution)/shard_map/transpose | solution.py:614
  10.9 139.2 %shard_map.305 = (bf16[4,128,768]{2,1,0:T(8,128)(2,1)}, bf16[4,128,768]{2,1,0:T(8,128)(2,1)}, bf16[4,96,768]{2,1,0:T(8,128)(2,1)}, bf16[3,96,1024]{2,1,0:T(8,128...) custom-call(s32[4]{0:T(128)} %refs_0_.1, f32[16,1024]{1,0:T(8,128)} %concatenate.7.refs_1_, ...), custom_call_target="tpu_custom_call" | custom-call | tf_op jit(solution)/shard_map/pallas_call | solution.py:639
  150.1 2.7 %copy.43 = bf16[128,4,768]{2,1,0:T(4,128)(2,1)} copy(bf16[128,4,768]{2,0,1:T(8,128)(2,1)} %bitcast.73) | data formatting | bytes 1572864
  152.8 1.5 copy.44
  154.3 0.6 fusion
  154.9 0.1 reshape.112
  155.0 0.5 fusion.1
  155.5 0.1 convert_element_type.11
  155.6 1.0 slice_bitcast_fusion
  156.7 0.4 copy-done.2
  157.0 0.1 copy.45
  157.2 0.8 copy.51
  158.0 1.5 reshape.131
  159.5 1.1 bitcast_convert_fusion
  (14 shorter events, 0.0 us)
Async XLA Ops:
  150.0 2.7 %copy-start = (bf16[4,128,768]{2,1,0:T(8,128)(2,1)S(1)}, bf16[4,128,768]{2,1,0:T(8,128)(2,1)}, u32[]{:S(2)}) copy-start(bf16[4,128,768]{2,1,0:T(8,128)(2,1)} %get-tuple-element.24) | copy-start | bytes 2359300
  152.8 1.5 copy-start.4
  152.8 2.8 %copy-start.3 = (bf16[4,96,768]{2,1,0:T(8,128)(2,1)S(1)}, bf16[4,96,768]{2,1,0:T(8,128)(2,1)}, u32[]{:S(2)}) copy-start(bf16[4,96,768]{2,1,0:T(8,128)(2,1)} %get-tuple-element.25) | copy-start | bytes 1769476
  155.6 1.4 copy-start.2
  158.0 1.5 copy-start.1
